TPU v7x, 32 devices: a whole 2x2x4 slice. The times are simulated.
32 devices in a mesh: dp: 16 (over z, x, core), expert: 2 (over y).
Axes of the slice: x: 2, y: 2, z: 4, core: 2. Of those that a mesh axis runs over, the one named last changes fastest.
Arguments:
- tokens: bfloat16 [2048, 2048], P('dp'), may hold values from -6 to 6
- routes: int32 [2048, 8], P('dp'), may hold values from 0 to 15, all different within a row; in each aligned block of 128 rows (0 to 127, 128 to 255, ...) at most 64 rows name the same one
- kept_mask: int32 [2048, 8], P('dp'), may hold values from 0 to 1, as said below
- gate_probs: float32 [2048, 8], P('dp'), may hold values from 0.05 to 0.5
- output_grad: bfloat16 [2048, 2048], P('dp'), may hold values from -96 to 96
- w_gate: bfloat16 [16, 2048, 1024], P('dp', None, 'expert'), may hold values from -0.125 to 0.125
- w_up: bfloat16 [16, 2048, 1024], P('dp', None, 'expert'), may hold values from -0.125 to 0.125
- w_down: bfloat16 [16, 1024, 2048], P('dp', 'expert'), may hold values from -0.1875 to 0.1875
Outputs:
- output: bfloat16 [2048, 2048], P('dp', 'expert')
- input_grad: bfloat16 [2048, 2048], P('dp', 'expert')
- grad_gate: bfloat16 [16, 2048, 1024], P('dp', None, 'expert')
- grad_up: bfloat16 [16, 2048, 1024], P('dp', None, 'expert')
- grad_down: bfloat16 [16, 1024, 2048], P('dp', 'expert')
Inputs may be any that keep to these rules, and one draw needn't show every extreme that they name: `routes`: each row names 8 different experts, and the 128 rows of each index of dp name every expert exactly 64 times. `kept_mask`: the share of kept entries varies along the tokens.
All inputs are finite; a program needn't handle non-finite values.
Results may differ from a plain program's by a relative error of at most 0.0064.
Values may be sent and summed in bfloat16 or wider, within the bound.
No kernel may reach another device: no remote copies, remote signals or barrier semaphores. Data moves between devices by JAX's collectives and lax.ppermute only.
A program may use at most 128 MiB of HBM per device.

v0:
```python
import jax
import jax.numpy as jnp
from jax import lax
from jax.sharding import PartitionSpec as P


def silu_parts(gate_val):
    sigmoid_val = jax.nn.sigmoid(gate_val)
    return (gate_val * sigmoid_val, sigmoid_val * (1.0 + gate_val * (1.0 - sigmoid_val)))


def slot_layout(routes, experts):
    tok_rows, top_count = routes.shape
    pair_count = tok_rows * top_count
    flat_routes = routes.reshape(pair_count)
    onehot = (flat_routes[:, None] == jnp.arange(experts, dtype=jnp.int32)[None, :]).astype(
        jnp.int32
    )
    before = jnp.cumsum(onehot, axis=0) - onehot
    slot_index = jnp.sum(before * onehot, axis=1)
    capacity = pair_count // experts
    dest_index = flat_routes * capacity + slot_index
    source = (
        jnp.zeros((pair_count,), jnp.int32)
        .at[dest_index]
        .set(jnp.arange(pair_count, dtype=jnp.int32))
    )
    return (dest_index, source, onehot)


def to_experts(rows_in, dp_size, local_experts):
    capacity = rows_in.shape[1]
    width = rows_in.shape[2]
    grouped = rows_in.reshape(dp_size, local_experts, capacity, width)
    return jnp.swapaxes(grouped, 0, 1).reshape(local_experts, dp_size * capacity, width)


def from_experts(values, dp_size):
    local_experts, slot_total, width = values.shape
    capacity = slot_total // dp_size
    grouped = values.reshape(local_experts, dp_size, capacity, width)
    return jnp.swapaxes(grouped, 0, 1).reshape(dp_size * local_experts, capacity, width)


def combine(back_rows, dest_index, factor, tok_rows, top_count):
    width = back_rows.shape[2]
    picked = back_rows.reshape(-1, width)[dest_index].astype(jnp.float32) * factor[:, None]
    return jnp.sum(picked.reshape(tok_rows, top_count, width), axis=1)


def per_device(tokens, routes, kept_mask, gate_probs, output_grad, w_gate, w_up, w_down):
    dp_size = lax.axis_size("dp")
    part_count = lax.axis_size("expert")
    local_experts, model_width, hidden_part = w_gate.shape
    experts = local_experts * dp_size
    tok_rows, top_count = routes.shape
    capacity = tok_rows * top_count // experts
    col_width = model_width // part_count
    dest_index, source, onehot = slot_layout(routes, experts)
    keep_float = kept_mask.reshape(-1).astype(jnp.float32)
    weight_flat = keep_float * gate_probs.reshape(-1)
    src_token = source // top_count
    src_keep = keep_float[source]
    src_weight = weight_flat[source]
    col_start = lax.axis_index("expert") * col_width
    token_src = lax.dynamic_slice_in_dim(tokens, col_start, col_width, 1)
    cot_src = lax.dynamic_slice_in_dim(output_grad, col_start, col_width, 1)
    send_width = token_src.shape[1]
    rows_send = (token_src[src_token].astype(jnp.float32) * src_keep[:, None]).astype(jnp.bfloat16)
    rows_send = rows_send.reshape(experts, capacity, send_width)
    cot_send = (cot_src[src_token].astype(jnp.float32) * src_weight[:, None]).astype(jnp.bfloat16)
    cot_send = cot_send.reshape(experts, capacity, send_width)
    totals = jnp.sum(onehot.astype(jnp.float32) * keep_float[:, None], axis=0)
    totals = lax.psum(totals, "dp")
    kept_count = lax.dynamic_slice_in_dim(
        totals, lax.axis_index("dp") * local_experts, local_experts
    )
    rows_in = lax.all_to_all(rows_send, "dp", split_axis=0, concat_axis=0, tiled=True)
    cot_in = lax.all_to_all(cot_send, "dp", split_axis=0, concat_axis=0, tiled=True)
    rows_in = lax.all_gather(rows_in, "expert", axis=2, tiled=True)
    cot_in = lax.all_gather(cot_in, "expert", axis=2, tiled=True)
    expert_in = to_experts(rows_in, dp_size, local_experts)
    cot_full = to_experts(cot_in, dp_size, local_experts)
    down_cols = lax.all_to_all(w_down, "expert", split_axis=2, concat_axis=1, tiled=True)
    gate_rows, up_rows = (
        lax.all_to_all(w_gate, "expert", split_axis=1, concat_axis=2, tiled=True),
        lax.all_to_all(w_up, "expert", split_axis=1, concat_axis=2, tiled=True),
    )
    gate_val = jnp.einsum("lsd,ldh->lsh", expert_in, w_gate, preferred_element_type=jnp.float32)
    up_val = jnp.einsum("lsd,ldh->lsh", expert_in, w_up, preferred_element_type=jnp.float32)
    act_val, act_slope = silu_parts(gate_val)
    hidden = (act_val * up_val).astype(jnp.bfloat16)
    expert_out = jnp.einsum(
        "lsh,lhc->lsc",
        lax.all_gather(hidden, "expert", axis=2, tiled=True),
        down_cols,
        preferred_element_type=jnp.float32,
    ).astype(jnp.bfloat16)
    out_back = lax.all_to_all(
        from_experts(expert_out, dp_size), "dp", split_axis=0, concat_axis=0, tiled=True
    )
    output = combine(out_back, dest_index, weight_flat, tok_rows, top_count).astype(jnp.bfloat16)
    d_hidden = jnp.einsum("lsd,lhd->lsh", cot_full, w_down, preferred_element_type=jnp.float32)
    d_gate = (d_hidden * up_val * act_slope).astype(jnp.bfloat16)
    d_up = (d_hidden * act_val).astype(jnp.bfloat16)
    inv_count = (1.0 / jnp.maximum(kept_count, 1.0))[:, None, None]
    grad_down = (
        jnp.einsum("lsh,lsd->lhd", hidden, cot_full, preferred_element_type=jnp.float32) * inv_count
    ).astype(jnp.bfloat16)
    grad_gate = (
        jnp.einsum("lsd,lsh->ldh", expert_in, d_gate, preferred_element_type=jnp.float32)
        * inv_count
    ).astype(jnp.bfloat16)
    grad_up = (
        jnp.einsum("lsd,lsh->ldh", expert_in, d_up, preferred_element_type=jnp.float32) * inv_count
    ).astype(jnp.bfloat16)
    running = jnp.einsum(
        "lsh,lch->lsc",
        lax.all_gather(d_gate, "expert", axis=2, tiled=True),
        gate_rows,
        preferred_element_type=jnp.float32,
    )
    d_rows = (
        running
        + jnp.einsum(
            "lsh,lch->lsc",
            lax.all_gather(d_up, "expert", axis=2, tiled=True),
            up_rows,
            preferred_element_type=jnp.float32,
        )
    ).astype(jnp.bfloat16)
    grad_back = lax.all_to_all(
        from_experts(d_rows, dp_size), "dp", split_axis=0, concat_axis=0, tiled=True
    )
    input_grad = combine(grad_back, dest_index, keep_float, tok_rows, top_count).astype(
        jnp.bfloat16
    )
    return (output, input_grad, grad_gate, grad_up, grad_down)


def solution(mesh):
    placed = (
        P("dp", None),
        P("dp", None),
        P("dp", None),
        P("dp", None),
        P("dp", None),
        P("dp", None, "expert"),
        P("dp", None, "expert"),
        P("dp", "expert", None),
    )
    return jax.shard_map(
        per_device,
        mesh=mesh,
        in_specs=placed,
        out_specs=(
            P("dp", "expert"),
            P("dp", "expert"),
            P("dp", None, "expert"),
            P("dp", None, "expert"),
            P("dp", "expert", None),
        ),
        check_vma=False,
    )
```

profile of v0, /device:TPU:0, one launch (start us, length us, event | category | flops | bytes accessed | tf_op | source)
XLA Modules:
  0.0 520.5 jit_solution(6219567556749429950)
XLA Ops:
  9.9 4.5 reduce-window.6
  14.9 4.3 scatter_custom_fusion
  19.3 4.5 gather_fusion.1
  29.8 7.5 %all-to-all-start = ((bf16[16,64,1024]{2,1,0:T(8,128)(2,1)}), bf16[16,64,1024]{2,1,0:T(8,128)(2,1)}, u32[]{:S(2)}, u32[]{:S(2)}) async-start(bf16[16,64,1024]{2,1,0:T(8,128)(2,1)} %fusion.3), calls=%async_computation | async-start | bytes 4194304 | tf_op jit(solution)/shard_map/all_to_all | solution.py:78
  37.6 4.5 gather_fusion.4
  46.2 32.2 %all-to-all-done = bf16[16,64,1024]{2,1,0:T(8,128)(2,1)} async-done(((bf16[16,64,1024]{2,1,0:T(8,128)(2,1)}), bf16[16,64,1024]{2,1,0:T(8,128)(2,1)}, u32[]{:S(2)}, u32[]{:S(2)}) %all-to-all-start) | async-done | bytes 2097184 | tf_op jit(solution)/shard_map/all_to_all | solution.py:78
  79.0 58.4 %all_to_all.65 = bf16[16,64,1024]{2,1,0:T(8,128)(2,1)} all-to-all(bf16[16,64,1024]{2,1,0:T(8,128)(2,1)S(1)} %fusion.1), channel_id=1, replica_groups=mesh['dp'=16,'expert'=2] {'dp'}, dimensions={0} | all-to-all | bytes 4194304 | tf_op jit(solution)/shard_map/all_to_all | solution.py:79
  137.6 4.3 all-gather.9.cloned.1.call-done
  142.0 6.6 %fusion.9 = f32[1024,512]{1,0:T(8,128)} fusion(bf16[1024,2048]{1,0:T(8,128)(2,1)} %bitcast.106, bf16[1,2048,512]{2,1,0:T(8,128)(2,1)} %param.14), kind=kOutput, calls=%fused_computation.24 | convolution fusion | flops 2147483648 | bytes 8388608 | tf_op jit(solution)/shard_map/lsd,ldh->lsh/dot_general | solution.py:90
  152.2 48.0 %all-gather.11.cloned.1.call-done = bf16[16,64,2048]{2,1,0:T(8,128)(2,1)} async-done(((bf16[16,64,1024]{2,1,0:T(8,128)(2,1)}), bf16[16,64,2048]{2,1,0:T(8,128)(2,1)}) %all-gather.11.cloned.1.call-update) | async-done | bytes 4194320 | tf_op jit(solution)/shard_map/all_gather | solution.py:81
  200.3 8.8 %multiply_convert_fusion.3 = (bf16[1024,512]{1,0:T(8,128)(2,1)}, bf16[1024,512]{1,0:T(8,128)(2,1)}, bf16[1024,512]{1,0:T(8,128)(2,1)}) fusion(f32[1024,512]{1,0:T(8,128)} %fusion.11, f32[1024,512]{1,0:T(8,128)} %fusion.9, bf16[1024,2048]{1,0:T(8,128)(2,1)} %bitcast.110, bf16[1,512,2048]{2,1,0:T(8,128)(2,1)} %param.15), kind=kOutput, calls=%fused_computation.28 | convolution fusion | flops 2155347968 | bytes 13631488 | tf_op jit(solution)/shard_map/lsd,lhd->lsh/dot_general | solution.py:103
  209.1 18.5 %copy.62 = bf16[1,2048,512]{2,0,1:T(2,128)(2,1)} copy(bf16[1,2048,512]{2,1,0:T(8,128)(2,1)S(1)} %copy-done.1) | data formatting | bytes 4194304 | tf_op args[5]
  228.1 14.1 %reduce.1 = bf16[2048,512]{1,0:T(8,128)(2,1)S(1)} reduce(bf16[2048,1,512]{2,1,0:T(2,128)(2,1)} %bitcast.85, bf16[]{:T(256)} %broadcast.117), dimensions={1}, to_apply=%bitcast.82.reduce_sub_computation | reduce | bytes 4194306
  249.1 7.5 %copy.61 = bf16[1,2048,512]{2,0,1:T(2,128)(2,1)} copy(bf16[1,2048,512]{2,1,0:T(8,128)(2,1)} %param.14) | data formatting | bytes 4194304 | tf_op args[6]
  256.6 15.4 %reduce.2 = bf16[2048,512]{1,0:T(8,128)(2,1)} reduce(bf16[2048,1,512]{2,1,0:T(2,128)(2,1)} %bitcast.90, bf16[]{:T(256)} %broadcast.117), dimensions={1}, to_apply=%bitcast.81.reduce_sub_computation | reduce | bytes 4194306
  275.8 10.0 %all-to-all-done.4 = bf16[2,2,262144]{2,1,0:T(2,128)(2,1)S(1)} async-done(((bf16[2,2,262144]{2,1,0:T(2,128)(2,1)}), bf16[2,2,262144]{2,1,0:T(2,128)(2,1)S(1)}, u32[]{:S(2)}, u32[]{:S(2)}) %all-to-all-start.4) | async-done | bytes 2097184 | tf_op jit(solution)/shard_map/all_to_all | solution.py:86
  285.8 4.8 all-to-all-start.5
  290.6 10.8 %copy.45 = bf16[1,512,2048]{1,0,2:T(2,128)(2,1)} copy(bf16[1,512,2048]{2,1,0:T(8,128)(2,1)} %param.15) | data formatting | bytes 4194304 | tf_op args[7]
  301.4 15.4 %reduce = bf16[2048,512]{1,0:T(8,128)(2,1)} reduce(bf16[2048,1,512]{2,1,0:T(2,128)(2,1)} %bitcast.86, bf16[]{:T(256)} %broadcast.117), dimensions={1}, to_apply=%bitcast.56.reduce_sub_computation | reduce | bytes 4194306
  328.8 4.2 all-to-all-start.1
  333.0 4.3 reshape.302
  345.4 6.5 %fusion.25 = f32[1024,1024]{1,0:T(8,128)} fusion(bf16[1024,1024]{1,0:T(8,128)(2,1)} %all-gather.15.cloned.1.call-done, bf16[1024,1024]{0,1:T(8,128)(2,1)} %bitcast.98), kind=kOutput, calls=%fused_computation.66 | convolution fusion | flops 2147483648 | bytes 8388608 | tf_op jit(solution)/shard_map/lsh,lch->lsc/dot_general | solution.py:117
  351.9 7.1 %add_convert_fusion = bf16[1024,1024]{1,0:T(8,128)(2,1)} fusion(f32[1024,1024]{1,0:T(8,128)} %fusion.25, bf16[1024,1024]{1,0:T(8,128)(2,1)} %all-gather.17.cloned.1.call-done, bf16[1024,1024]{0,1:T(8,128)(2,1)} %bitcast.99), kind=kOutput, calls=%fused_computation.18 | convolution fusion | flops 2149580800 | bytes 10485760 | tf_op jit(solution)/shard_map/lsh,lch->lsc/dot_general | solution.py:125
  360.4 5.6 %all-to-all-start.6 = ((bf16[16,64,1024]{2,1,0:T(8,128)(2,1)}), bf16[16,64,1024]{2,1,0:T(8,128)(2,1)S(1)}, u32[]{:S(2)}, u32[]{:S(2)}) async-start(bf16[16,64,1024]{2,1,0:T(8,128)(2,1)} %bitcast.97), calls=%async_computation.6 | async-start | bytes 4194304 | tf_op jit(solution)/shard_map/all_to_all | solution.py:132
  366.6 4.3 reshape.298
  379.1 24.0 %all-gather.13.cloned.1.call-done = bf16[1024,1024]{1,0:T(8,128)(2,1)} async-done(((bf16[1024,512]{1,0:T(8,128)(2,1)}), bf16[1024,1024]{1,0:T(8,128)(2,1)}) %all-gather.13.cloned.1.call-update) | async-done | bytes 2097168 | tf_op jit(solution)/shard_map/all_gather | solution.py:95
  403.1 5.9 %convolution_convert_fusion = bf16[1024,1024]{1,0:T(8,128)(2,1)} fusion(bf16[1024,1024]{1,0:T(8,128)(2,1)} %all-gather.13.cloned.1.call-done, bf16[1024,1024]{1,0:T(8,128)(2,1)} %bitcast.100), kind=kOutput, calls=%fused_computation.33 | convolution fusion | flops 2148532224 | bytes 6291456 | tf_op jit(solution)/shard_map/lsh,lhc->lsc/dot_general | solution.py:93
  409.0 9.5 %all-to-all-start.2 = ((bf16[16,64,1024]{2,1,0:T(8,128)(2,1)}), bf16[16,64,1024]{2,1,0:T(8,128)(2,1)}, u32[]{:S(2)}, u32[]{:S(2)}) async-start(bf16[16,64,1024]{2,1,0:T(8,128)(2,1)} %bitcast.96), calls=%async_computation.2 | async-start | bytes 4194304 | tf_op jit(solution)/shard_map/all_to_all | solution.py:99
  418.6 62.3 %psum.7 = f32[16]{0:T(128)S(1)} all-reduce(f32[16]{0:T(128)S(1)} %fusion.17), channel_id=1, replica_groups=mesh['dp'=16,'expert'=2] {'dp'}, use_global_device_ids=true, to_apply=%region_7.8 | all-reduce | flops 16 | bytes 128 | tf_op jit(solution)/shard_map/psum | solution.py:74
  482.4 6.1 %fusion.6 = bf16[1,512,2048]{2,1,0:T(8,128)(2,1)} fusion(bf16[1024,512]{1,0:T(8,128)(2,1)S(1)} %copy-done.4, bf16[1024,2048]{1,0:T(8,128)(2,1)} %bitcast.111, f32[]{:T(128)} %bitcast.23), kind=kOutput, calls=%fused_computation.21 | convolution fusion | flops 2149580800 | bytes 7340036 | tf_op jit(solution)/shard_map/lsh,lsd->lhd/dot_general | solution.py:108
  496.0 5.3 %gather_fusion.5 = bf16[1024,1024]{1,0:T(8,128)(2,1)} fusion(bf16[1024,1024]{1,0:T(8,128)(2,1)S(1)} %bitcast.84, s32[1024]{0:T(1024)S(1)} %broadcast_clamp_fusion), kind=kCustom, calls=%fused_computation.5 | custom fusion | bytes 4198400 | tf_op jit(solution)/shard_map/gather | solution.py:47
  505.0 6.8 %gather_fusion.2 = bf16[1024,1024]{1,0:T(8,128)(2,1)S(1)} fusion(bf16[1024,1024]{1,0:T(8,128)(2,1)} %bitcast.11, s32[1024]{0:T(1024)S(1)} %broadcast_clamp_fusion), kind=kCustom, calls=%fused_computation.2 | custom fusion | bytes 4198400 | tf_op jit(solution)/shard_map/gather | solution.py:47
  (90 shorter events, 73.2 us)
Async XLA Ops:
  19.3 4.6 copy-start.5
  19.3 4.6 copy-start.6
  29.8 7.6 %copy-start.7 = (f32[128,8]{0,1:T(8,128)S(1)}, f32[128,8]{0,1:T(8,128)}, u32[]{:S(2)}) copy-start(f32[128,8]{0,1:T(8,128)} %param.11) | copy-start | bytes 12292
  29.8 48.7 %all-to-all-start = ((bf16[16,64,1024]{2,1,0:T(8,128)(2,1)}), bf16[16,64,1024]{2,1,0:T(8,128)(2,1)}, u32[]{:S(2)}, u32[]{:S(2)}) async-start(bf16[16,64,1024]{2,1,0:T(8,128)(2,1)} %fusion.3), calls=%async_computation | async-start | bytes 4194304 | tf_op jit(solution)/shard_map/all_to_all | solution.py:78
  37.3 104.6 %all-gather.9.cloned.1.call-start = ((), (), s32[]{:S(2)}) async-start(), calls=%async_computation.7 | async-start | bytes 6291456 | tf_op jit(solution)/shard_map/all_gather | solution.py:80
  78.5 121.8 %all-gather.11.cloned.1.call-start = ((), (), s32[]{:S(2)}) async-start(), calls=%async_computation.8 | async-start | bytes 6291456 | tf_op jit(solution)/shard_map/all_gather | solution.py:81
  137.4 208.0 %all-gather.15.cloned.1.call-start = ((), (), s32[]{:S(2)}) async-start(), calls=%async_computation.10 | async-start | bytes 3145728 | tf_op jit(solution)/shard_map/all_gather | solution.py:119
  142.0 6.6 %copy-start.1 = (bf16[1,2048,512]{2,1,0:T(8,128)(2,1)S(1)}, bf16[1,2048,512]{2,1,0:T(8,128)(2,1)}, u32[]{:S(2)}) copy-start(bf16[1,2048,512]{2,1,0:T(8,128)(2,1)} %param.13) | copy-start | bytes 6291460
  142.0 6.6 %copy-start.9 = (bf16[16,64,2048]{2,1,0:T(8,128)(2,1)S(1)}, bf16[16,64,2048]{2,1,0:T(8,128)(2,1)}, u32[]{:S(2)}) copy-start(bf16[16,64,2048]{2,1,0:T(8,128)(2,1)} %all-gather.9.cloned.1.call-done) | copy-start | bytes 12582916
  244.7 41.0 %all-to-all-start.4 = ((bf16[2,2,262144]{2,1,0:T(2,128)(2,1)}), bf16[2,2,262144]{2,1,0:T(2,128)(2,1)S(1)}, u32[]{:S(2)}, u32[]{:S(2)}) async-start(bf16[2,2,262144]{2,1,0:T(2,128)(2,1)} %reshape.299), calls=%async_computation.4 | async-start | bytes 4194304 | tf_op jit(solution)/shard_map/all_to_all | solution.py:86
  248.5 103.4 %all-gather.17.cloned.1.call-start = ((), (), s32[]{:S(2)}) async-start(), calls=%async_computation.11 | async-start | bytes 3145728 | tf_op jit(solution)/shard_map/all_gather | solution.py:127
  285.8 43.0 %all-to-all-start.5 = ((bf16[2,2,262144]{2,1,0:T(2,128)(2,1)}), bf16[2,2,262144]{2,1,0:T(2,128)(2,1)}, u32[]{:S(2)}, u32[]{:S(2)}) async-start(bf16[2,2,262144]{2,1,0:T(2,128)(2,1)} %reshape.301), calls=%async_computation.5 | async-start | bytes 4194304 | tf_op jit(solution)/shard_map/all_to_all | solution.py:87
  328.8 30.2 %all-to-all-start.1 = ((bf16[2,2,262144]{2,1,0:T(2,128)(2,1)}), bf16[2,2,262144]{2,1,0:T(2,128)(2,1)S(1)}, u32[]{:S(2)}, u32[]{:S(2)}) async-start(bf16[2,2,262144]{2,1,0:T(2,128)(2,1)} %reshape.297), calls=%async_computation.1 | async-start | bytes 4194304 | tf_op jit(solution)/shard_map/all_to_all | solution.py:84
  359.1 1.3 copy-start
  360.4 48.6 %all-to-all-start.6 = ((bf16[16,64,1024]{2,1,0:T(8,128)(2,1)}), bf16[16,64,1024]{2,1,0:T(8,128)(2,1)S(1)}, u32[]{:S(2)}, u32[]{:S(2)}) async-start(bf16[16,64,1024]{2,1,0:T(8,128)(2,1)} %bitcast.97), calls=%async_computation.6 | async-start | bytes 4194304 | tf_op jit(solution)/shard_map/all_to_all | solution.py:132
  366.0 37.1 %all-gather.13.cloned.1.call-start = ((), (), s32[]{:S(2)}) async-start(), calls=%async_computation.9 | async-start | bytes 3145728 | tf_op jit(solution)/shard_map/all_gather | solution.py:95
  409.0 71.9 %copy-start.8 = (s32[128,8]{0,1:T(8,128)S(1)}, s32[128,8]{0,1:T(8,128)}, u32[]{:S(2)}) copy-start(s32[128,8]{0,1:T(8,128)} %param.10) | copy-start | bytes 12292
  409.0 73.3 %copy-start.4 = (bf16[1024,512]{1,0:T(8,128)(2,1)S(1)}, bf16[1024,512]{1,0:T(8,128)(2,1)}, u32[]{:S(2)}) copy-start(bf16[1024,512]{1,0:T(8,128)(2,1)} %get-tuple-element.7) | copy-start | bytes 3145732
  409.0 96.0 %all-to-all-start.2 = ((bf16[16,64,1024]{2,1,0:T(8,128)(2,1)}), bf16[16,64,1024]{2,1,0:T(8,128)(2,1)}, u32[]{:S(2)}, u32[]{:S(2)}) async-start(bf16[16,64,1024]{2,1,0:T(8,128)(2,1)} %bitcast.96), calls=%async_computation.2 | async-start | bytes 4194304 | tf_op jit(solution)/shard_map/all_to_all | solution.py:99
  482.3 6.1 %copy-start.3 = (bf16[1024,512]{1,0:T(8,128)(2,1)S(1)}, bf16[1024,512]{1,0:T(8,128)(2,1)}, u32[]{:S(2)}) copy-start(bf16[1024,512]{1,0:T(8,128)(2,1)} %get-tuple-element.5) | copy-start | bytes 3145732
  482.3 6.1 %copy-start.10 = (bf16[16,64,2048]{2,1,0:T(8,128)(2,1)S(1)}, bf16[16,64,2048]{2,1,0:T(8,128)(2,1)}, u32[]{:S(2)}) copy-start(bf16[16,64,2048]{2,1,0:T(8,128)(2,1)} %all-gather.9.cloned.1.call-done) | copy-start | bytes 12582916
  488.4 3.8 copy-start.2
Sparse Core Ops, SparseCore 0:
  78.6 63.2 all-gather.8
  143.5 56.7 all-gather.10
  209.2 33.1 all-gather.14
  250.6 50.2 all-gather.16
  368.1 34.9 all-gather.12
where the time goes:
time: 528 us; the launch traced here: 521 us
  blocking collectives  121 us (23%)
  waiting for transfers between devices  119 us (23%)
  local copies, waits for them, and re-layouts  118 us (22%)
  other arithmetic  58.9 us (11%)
  matrix products  52.2 us (10%)
  starting transfers between devices  36 us (7%)
  between operations  14.9 us (3%)
    unnamed x37, local copies, waits for them, and re-layouts  72.4 us
    psum x1, blocking collectives, per_device(): totals = lax.psum(totals, 'dp')  62.3 us
    all_to_all x1, blocking collectives, per_device(): lax.all_to_all(cot_send, 'dp', split_axis=0, concat_axis=0, tiled=True)  58.4 us
    all_gather x1, waiting for transfers between devices, per_device(): cot_in = lax.all_gather(cot_in, 'expert', axis=2, tiled=True)  48 us
    unnamed x3, other arithmetic  44.9 us
    all_to_all x1, waiting for transfers between devices, per_device(): lax.all_to_all(rows_send, 'dp', split_axis=0, concat_axis=0, tiled=True)  32.2 us
    all_gather x1, waiting for transfers between devices, per_device(): lax.all_gather(hidden, 'expert', axis=2, tiled=True)  24 us
    gather x2, local copies, waits for them, and re-layouts, combine(): back_rows.reshape(-1, width)[dest_index].astype(jnp.float32)  12.2 us
  transfers between devices with their start and end apart: 11, of which 5 were waited for; matrix products, arithmetic and copies ran while one was open for 36% of the time, Pallas kernels for 0%

commit v1 on v0

--- a/solution.py
+++ b/solution.py
@@ -1,6 +1,11 @@
+import functools
+import math
+
 import jax
 import jax.numpy as jnp
 from jax import lax
+from jax.experimental import pallas as pl
+from jax.experimental.pallas import tpu as pltpu
 from jax.sharding import PartitionSpec as P
 
 
@@ -48,7 +53,7 @@
     return jnp.sum(picked.reshape(tok_rows, top_count, width), axis=1)
 
 
-def per_device(tokens, routes, kept_mask, gate_probs, output_grad, w_gate, w_up, w_down):
+def routed_plan(tokens, routes, kept_mask, gate_probs, output_grad, w_gate, w_up, w_down):
     dp_size = lax.axis_size("dp")
     part_count = lax.axis_size("expert")
     local_experts, model_width, hidden_part = w_gate.shape
@@ -138,6 +143,321 @@
     return (output, input_grad, grad_gate, grad_up, grad_down)
 
 
+def swap(values, axis_name, bit):
+    size = lax.axis_size(axis_name)
+    return lax.ppermute(values, axis_name, [(i, i ^ bit) for i in range(size)])
+
+
+def shift(values, steps):
+    size = lax.axis_size("dp")
+    return lax.ppermute(values, "dp", [(i, (i + 4 * steps) % size) for i in range(size)])
+
+
+def cut_halves(part_ref, tokens, cots, mine, other):
+    rows = tokens.shape[0] // 2
+    own = pl.multiple_of(part_ref[0] * rows, rows)
+    rest = pl.multiple_of(rows - part_ref[0] * rows, rows)
+    for kind, values in enumerate((tokens, cots)):
+        mine[kind] = values[pl.ds(own, rows), :]
+        other[kind] = values[pl.ds(rest, rows), :]
+
+
+def own_halves(part_arg, tokens, cots):
+    shape = jax.ShapeDtypeStruct((2, tokens.shape[0] // 2, tokens.shape[1]), tokens.dtype)
+    vmem = pl.BlockSpec(memory_space=pltpu.VMEM)
+    return call_kernel(
+        cut_halves,
+        "own_halves",
+        [shape, shape],
+        [part_arg, tokens, cots],
+        in_specs=[pl.BlockSpec(memory_space=pltpu.SMEM), vmem, vmem],
+    )
+
+
+def gather_line(part_arg, tokens, cots, line):
+    mine, other = own_halves(part_arg, tokens, cots)
+    halves = [mine]
+    for _ in range(line - 1):
+        halves.append(shift(halves[-1], 1))
+    steps = []
+    for step, half in enumerate(halves):
+        rest = swap(half, "expert", 1) if step else other
+        across = swap(half, "dp", 2)
+        if step:
+            last = (swap(rest[0], "dp", 2), swap(across[1], "expert", 1))
+        else:
+            last = tuple(swap(across[kind], "expert", 1) for kind in range(2))
+        pieces = (half, rest, across) + last
+        steps.append(pieces + tuple(swap(piece, "dp", 1) for piece in pieces))
+    return steps
+
+
+def gather_small(values, line):
+    lines = jnp.stack([values] + [shift(values, step) for step in range(1, line)])
+    pairs = jnp.stack([lines, swap(lines, "dp", 2)], axis=1)
+    return jnp.stack([pairs, swap(pairs, "dp", 1)], axis=2)
+
+
+def mxu(a, b, dims=((1,), (0,))):
+    return lax.dot_general(a, b, (dims, ((), ())), preferred_element_type=jnp.float32)
+
+
+def add_to(target, *terms):
+    target[...] = sum(term.astype(jnp.float32) for term in terms).astype(jnp.bfloat16)
+
+
+def add_cores(keep, got, *refs):
+    away_out, away_grad, home = refs
+    add_to(away_out, keep[0, 1], got[0, 1])
+    add_to(away_grad, keep[1, 1], got[1, 1])
+    add_to(home, keep[:, 0], got[:, 0])
+
+
+def add_first(home, away_out, away_grad, *refs):
+    last_out, last_grad = refs[-2:]
+    add_to(last_out, home[0, 1], away_out[1])
+    add_to(last_grad, home[1, 1], away_grad[1])
+
+
+def add_last(home, away_out, away_grad, last_out, last_grad, *refs):
+    total = refs[-1]
+    add_to(total.at[0], home[0, 0], away_out[0], last_out[...])
+    add_to(total.at[1], home[1, 0], away_grad[0], last_grad[...])
+
+
+def call_kernel(kernel, name, shapes, args, flops=0, vmem=8 * 2**20, **options):
+    space = pl.BlockSpec(memory_space=pltpu.VMEM)
+    moved = sum(math.prod(a.shape) * a.dtype.itemsize for a in [*args, *shapes])
+    return pl.pallas_call(
+        kernel,
+        out_shape=shapes,
+        in_specs=options.pop("in_specs", [space] * len(args)),
+        out_specs=options.pop("out_specs", [space] * len(shapes)),
+        compiler_params=pltpu.CompilerParams(vmem_limit_bytes=vmem),
+        cost_estimate=pl.CostEstimate(flops=flops, bytes_accessed=moved, transcendentals=0),
+        name=name,
+        **options,
+    )(*args)
+
+
+def send_home(keep, send, step):
+    def array(*shape):
+        return jax.ShapeDtypeStruct(shape, jnp.bfloat16)
+
+    rows, columns = keep.shape[3:]
+    pair, single = array(2, rows, columns), array(rows, columns)
+    got = swap(send, "dp", 1)
+    away_out, away_grad, home = call_kernel(
+        add_cores, "add_cores", [pair, pair, array(2, 2, rows, columns)], [keep, got]
+    )
+    away = (swap(away_out, "dp", 2), swap(away_grad, "expert", 1))
+    lasts = call_kernel(add_first, "add_first", [single, single], [home, *away])
+    last = (swap(lasts[0], "expert", 1), swap(lasts[1], "dp", 2))
+    total = call_kernel(add_last, "add_last", [pair], [home, *away, *last])[0]
+    return shift(total, -step) if step else total
+
+
+def take_rows(kind, pick_ref, pieces, store):
+    for x in range(2):
+        for core in range(2):
+            half, rest, across, *last = pieces[5 * core : 5 * core + 5]
+            if x == 0:
+                block = jnp.concatenate([half[kind], rest[kind]], axis=0)
+            else:
+                block = jnp.concatenate([across[kind], last[kind][...]], axis=0)
+            store(2 * x + core, mxu(pick_ref[x, core], block))
+
+
+def spread_rows(kind, part, half, rows, place_ref, keep_ref, send_ref):
+    capacity = rows.shape[0] // 4
+    side = half ^ part
+    for x in range(2):
+        for core in range(2):
+            group = 2 * x + core
+            piece = rows[group * capacity : (group + 1) * capacity]
+            out = mxu(place_ref[x, core], piece).astype(jnp.bfloat16)
+            target = keep_ref if core == 0 else send_ref
+            if kind == 0:
+                target[kind, x, side] = out
+            else:
+                target[kind, side, x] = out
+
+
+def chunk_kernel(step, part_ref, pick_ref, place_ref, scale_ref, *refs):
+    sources, refs = refs[:13], refs[-30:]
+    outs, saved = refs[:2], refs[2:7]
+    kept, buffers, homes, sems = refs[7:12], refs[12:25], refs[25:27], refs[27:]
+    keep_ref, send_ref = homes
+    rows_ref, cot_ref, hidden_ref, d_gate_ref, d_up_ref = kept
+    pieces, (w_gate, w_up, w_down) = buffers[:10], buffers[10:]
+    rows, capacity = rows_ref.shape[0], pick_ref.shape[2]
+    loads = [
+        pltpu.make_async_copy(source, target, sems[0].at[i])
+        for i, (source, target) in enumerate(zip(sources, buffers))
+    ]
+    stores = [
+        pltpu.make_async_copy(source, target.at[pl.ds(step * rows, rows)], sems[1].at[i])
+        for i, (source, target) in enumerate(zip(kept, saved))
+    ]
+    sends = [
+        pltpu.make_async_copy(source.at[kind], target.at[kind], sems[2].at[kind, i])
+        for kind in range(2)
+        for i, (source, target) in enumerate(zip(homes, outs))
+    ]
+    for load in loads:
+        load.start()
+
+    def store_rows(group, found):
+        rows_ref[pl.ds(group * capacity, capacity), :] = found.astype(jnp.bfloat16)
+
+    def store_cot(group, found):
+        span = pl.ds(group * capacity, capacity)
+        cot_ref[span, :] = (found * scale_ref[span, :]).astype(jnp.bfloat16)
+
+    for load in loads[:10]:
+        load.wait()
+    take_rows(0, pick_ref, pieces, store_rows)
+    stores[0].start()
+    take_rows(1, pick_ref, pieces, store_cot)
+    stores[1].start()
+    for load in loads[10:]:
+        load.wait()
+    expert_in = rows_ref[...]
+    gate_val = mxu(expert_in, w_gate[...])
+    up_val = mxu(expert_in, w_up[...])
+    act_val, act_slope = silu_parts(gate_val)
+    hidden = (act_val * up_val).astype(jnp.bfloat16)
+    hidden_ref[...] = hidden
+    stores[2].start()
+    d_hidden = mxu(cot_ref[...], w_down[...], ((1,), (1,)))
+    d_gate = (d_hidden * up_val * act_slope).astype(jnp.bfloat16)
+    d_up = (d_hidden * act_val).astype(jnp.bfloat16)
+    d_gate_ref[...] = d_gate
+    d_up_ref[...] = d_up
+    stores[3].start()
+    stores[4].start()
+    width = w_down.shape[1] // 2
+    part = part_ref[0]
+    halves = [slice(half * width, (half + 1) * width) for half in range(2)]
+    for half, span in enumerate(halves):
+        out = (mxu(hidden, w_down[:, span]) * scale_ref[...]).astype(jnp.bfloat16)
+        spread_rows(0, part, half, out, place_ref, keep_ref, send_ref)
+    for send in sends[:2]:
+        send.start()
+    for half, span in enumerate(halves):
+        grad = mxu(d_gate, w_gate[span, :], ((1,), (1,))) + mxu(d_up, w_up[span, :], ((1,), (1,)))
+        spread_rows(1, part, half, grad.astype(jnp.bfloat16), place_ref, keep_ref, send_ref)
+    for send in sends[2:]:
+        send.start()
+    for copy in stores + sends:
+        copy.wait()
+
+
+def run_chunk(step, tables, sources, saved_shapes, saved):
+    def array(a):
+        return jax.ShapeDtypeStruct(a.shape, a.dtype)
+
+    def scratch(a):
+        return pltpu.VMEM(a.shape, a.dtype)
+
+    kinds, half_rows, model_width = sources[0].shape
+    home = jax.ShapeDtypeStruct((kinds, 2, 2, 2 * half_rows, model_width // 2), jnp.bfloat16)
+    vmem, hbm = pl.BlockSpec(memory_space=pltpu.VMEM), pl.BlockSpec(memory_space=pl.ANY)
+    rows = tables[-1].shape[0]
+    first_saved = len(tables) + len(sources)
+    return call_kernel(
+        functools.partial(chunk_kernel, step),
+        "chunk",
+        [home, home, *saved_shapes],
+        [*tables, *sources, *saved],
+        vmem=60 * 2**20,
+        flops=12 * rows * sources[-1].shape[0] * sources[-1].shape[1],
+        in_specs=[pl.BlockSpec(memory_space=pltpu.SMEM)]
+        + [vmem] * (len(tables) - 1)
+        + [hbm] * (len(sources) + len(saved)),
+        out_specs=[hbm] * (2 + len(saved_shapes)),
+        input_output_aliases={first_saved + i: 2 + i for i in range(len(saved))},
+        scratch_shapes=[pltpu.VMEM((rows, s.shape[1]), s.dtype) for s in saved_shapes]
+        + [scratch(source) for source in sources]
+        + [scratch(home)] * 2
+        + [pltpu.SemaphoreType.DMA(n) for n in ((len(sources),), (len(saved_shapes),), (2, 2))],
+    )
+
+
+def dense_plan(tokens, routes, kept_mask, gate_probs, output_grad, w_gate, w_up, w_down):
+    dp_size = lax.axis_size("dp")
+    line = dp_size // 4
+    tok_rows, top_count = routes.shape
+    capacity = tok_rows * top_count // dp_size
+    model_width = tokens.shape[1]
+    hidden_part = w_gate.shape[2]
+    rows = 4 * capacity
+    part = lax.axis_index("expert")
+    w_gate, w_up, w_down = w_gate[0], w_up[0], w_down[0]
+
+    table = jnp.concatenate(
+        [routes.T.astype(jnp.float32), kept_mask.T.astype(jnp.float32), gate_probs.T], axis=0
+    )
+    table = gather_small(table, line)
+    chosen, kept, probs = jnp.split(table, 3, axis=3)
+    expert = lax.axis_index("dp").astype(jnp.float32)
+    hit = jnp.where(chosen == expert, kept, 0.0)
+    used = jnp.sum(hit, axis=3)
+    weight = jnp.sum(hit * probs, axis=3)
+    kept_count = jnp.sum(used)
+    earlier = jnp.triu(jnp.ones((tok_rows, tok_rows), jnp.bfloat16), 1)
+    rank = jnp.einsum(
+        "sabt,tu->sabu", used.astype(jnp.bfloat16), earlier, preferred_element_type=jnp.float32
+    )
+    slots = jnp.arange(capacity, dtype=jnp.float32)[:, None]
+    pick = jnp.where(rank[..., None, :] == slots, used[..., None, :], 0.0)
+    row_weight = jnp.sum(pick * weight[..., None, :], axis=4).reshape(line, rows, 1)
+    pick = pick.astype(jnp.bfloat16)
+    place = jnp.swapaxes(pick, 3, 4)
+    pick_in = jnp.where(part == 0, pick, jnp.roll(pick, tok_rows // 2, axis=4))
+
+    part_arg = part.astype(jnp.int32).reshape(1)
+    pieces = gather_line(part_arg, tokens, output_grad, line)
+
+    def saved_array(width):
+        return jax.ShapeDtypeStruct((line * rows, width), jnp.bfloat16)
+
+    saved_shapes = [saved_array(model_width)] * 2 + [saved_array(hidden_part)] * 3
+    saved, returns = [], []
+
+    for step in range(line):
+        keep, send, *saved = run_chunk(
+            step,
+            [part_arg, pick_in[step], place[step], row_weight[step]],
+            [*pieces[step], w_gate, w_up, w_down],
+            saved_shapes,
+            saved,
+        )
+        returns.append(send_home(keep, send, step))
+    expert_in, cot_rows, hidden, d_gate, d_up = saved
+    inv_count = 1.0 / jnp.maximum(kept_count, 1.0)
+    by_row = ((0,), (0,))
+    grad_down = (mxu(hidden, cot_rows, by_row) * inv_count).astype(jnp.bfloat16)
+    grad_gate = (mxu(expert_in, d_gate, by_row) * inv_count).astype(jnp.bfloat16)
+    grad_up = (mxu(expert_in, d_up, by_row) * inv_count).astype(jnp.bfloat16)
+    results = sum(part_sum.astype(jnp.float32) for part_sum in returns).astype(jnp.bfloat16)
+    return (results[0], results[1], grad_gate[None], grad_up[None], grad_down[None])
+
+
+def per_device(tokens, routes, kept_mask, gate_probs, output_grad, w_gate, w_up, w_down):
+    dp_size = lax.axis_size("dp")
+    local_experts = w_gate.shape[0]
+    top_count = routes.shape[1]
+    dense = (
+        local_experts == 1
+        and lax.axis_size("expert") == 2
+        and dp_size % 4 == 0
+        and 2 * top_count >= dp_size
+    )
+    plan = dense_plan if dense else routed_plan
+    return plan(tokens, routes, kept_mask, gate_probs, output_grad, w_gate, w_up, w_down)
+
+
 def solution(mesh):
     placed = (
         P("dp", None),

time: 528 us -> 273 us (0.52)
  blocking collectives: 121 us -> 0 us
  local copies, waits for them, and re-layouts: 118 us -> 20.2 us
  Pallas kernels: 0 us -> 63.4 us
  other arithmetic: 58.9 us -> 3.63 us
  matrix products: 52.2 us -> 11.5 us
  starting transfers between devices: 36 us -> 54.4 us
  between operations: 14.9 us -> 2.45 us
  waiting for transfers between devices: 119 us -> 113 us
    ppermute x0 -> x66, waiting for transfers between devices: none -> 113 us  [the longest x57 66.6 us: swap(): return lax.ppermute(values, axis_name, [(i, i ^ bit) for i in range(size)])]
    all_gather x5 -> x0, waiting for transfers between devices: 76.3 us -> none  [the longest x1 48 us: per_device(): cot_in = lax.all_gather(cot_in, 'expert', axis=2, tiled=True)]
    pallas_call x0 -> x17, Pallas kernels: none -> 63.4 us  [call_kernel(): pl.pallas_call(kernel, out_shape=shapes, in_specs=options.pop('in_specs',...]
    psum x1 -> x0, blocking collectives: 62.3 us -> none  [per_device(): totals = lax.psum(totals, 'dp')]
    unnamed x37 -> x80, local copies, waits for them, and re-layouts: 72.4 us -> 10.7 us
    all_to_all x1 -> x0, blocking collectives: 58.4 us -> none  [per_device(): lax.all_to_all(cot_send, 'dp', split_axis=0, concat_axis=0, tiled=True)]
    ppermute x0 -> x66, starting transfers between devices: none -> 54.4 us  [the longest x57 40.1 us: swap(): return lax.ppermute(values, axis_name, [(i, i ^ bit) for i in range(size)])]
    unnamed x3 -> x0, other arithmetic: 44.9 us -> none
  transfers between devices with their start and end apart: 11 -> 66, of which waited for: 5 -> 19; matrix products, arithmetic and copies ran while one was open for 36% -> 8% of each run, Pallas kernels for 0% -> 24%
where the time goes in v1:
time: 273 us; the launch traced here: 269 us
  waiting for transfers between devices  113 us (41%)
  Pallas kernels  63.4 us (23%)
  starting transfers between devices  54.4 us (20%)
  local copies, waits for them, and re-layouts  20.2 us (7%)
  matrix products  11.5 us (4%)
  other arithmetic  3.63 us (1%)
    ppermute x57, waiting for transfers between devices, swap(): return lax.ppermute(values, axis_name, [(i, i ^ bit) for i in range(size)])  66.6 us
    pallas_call x17, Pallas kernels, call_kernel(): pl.pallas_call(kernel, out_shape=shapes, in_specs=options.pop('in_specs',...  63.4 us
    ppermute x9, waiting for transfers between devices, shift(): lax.ppermute(values, 'dp', [(i, (i + 4 * steps) % size) for i in range(si...  46.5 us
    ppermute x57, starting transfers between devices, swap(): return lax.ppermute(values, axis_name, [(i, i ^ bit) for i in range(size)])  40.1 us
    ppermute x9, starting transfers between devices, shift(): lax.ppermute(values, 'dp', [(i, (i + 4 * steps) % size) for i in range(si...  14.4 us
    dot_general x3, matrix products, mxu(): lax.dot_general(a, b, (dims, ((), ())), preferred_element_type=jnp.float32)  11.3 us
    unnamed x80, local copies, waits for them, and re-layouts  10.7 us
  transfers between devices with their start and end apart: 66, of which 19 were waited for; matrix products, arithmetic and copies ran while one was open for 8% of the time, Pallas kernels for 24%

profile of v1, /device:TPU:0, one launch (start us, length us, event | category | flops | bytes accessed | tf_op | source)
XLA Modules:
  0.0 268.7 jit_solution(6113407257351340503)
XLA Ops:
  2.0 4.0 %collective-permute-start.1 = (f32[24,128]{1,0:T(8,128)S(1)}, f32[24,128]{1,0:T(8,128)S(1)}, u32[]{:S(2)}, u32[]{:S(2)}) collective-permute-start(f32[24,128]{1,0:T(8,128)S(1)} %get-tuple-element.127), channel_id=1, source_target_pairs={{0,16},{2,18},{4,20},{6,22},{8,24},{10,26},{12,28},{14,30},{16,0},... | collective-permute-start | bytes 36872 | tf_op jit(solution)/shard_map/ppermute | solution.py:153
  7.6 2.2 collective-permute-start.2
  9.9 1.7 collective-permute-done
  13.1 2.6 collective-permute-done.3
  23.7 10.8 %collective-permute-done.18.refs_0_ = bf16[2,64,2048]{2,1,0:T(8,128)(2,1)S(1)} collective-permute-done((bf16[2,64,2048]{2,1,0:T(8,128)(2,1)S(1)}, bf16[2,64,2048]{2,1,0:T(8,128)(2,1)S(1)}, u32[]{:S(2)}, u32[]{:S(2)}) %collective-permute-start.18) | collective-permute-done | bytes 524320 | tf_op jit(solution)/shard_map/ppermute | solution.py:153
  41.6 4.7 %collective-permute-done.7.refs_4_ = bf16[64,2048]{1,0:T(8,128)(2,1)} collective-permute-done((bf16[64,2048]{1,0:T(8,128)(2,1)}, bf16[64,2048]{1,0:T(8,128)(2,1)}, u32[]{:S(2)}, u32[]{:S(2)}) %collective-permute-start.7) | collective-permute-done | bytes 262176 | tf_op jit(solution)/shard_map/ppermute | solution.py:148
  49.0 12.7 %collective-permute-done.6.refs_3_ = bf16[64,2048]{1,0:T(8,128)(2,1)S(1)} collective-permute-done((bf16[64,2048]{1,0:T(8,128)(2,1)S(1)}, bf16[64,2048]{1,0:T(8,128)(2,1)S(1)}, u32[]{:S(2)}, u32[]{:S(2)}) %collective-permute-start.6) | collective-permute-done | bytes 262176 | tf_op jit(solution)/shard_map/ppermute | solution.py:148
  68.1 12.3 %chunk.4 = (bf16[2,2,2,128,1024]{4,3,2,1,0:T(8,128)(2,1)}, bf16[2,2,2,128,1024]{4,3,2,1,0:T(8,128)(2,1)}, bf16[1024,2048]{1,0:T(8,128)(2,1)}, bf16[1024,2048]{1,...) custom-call(s32[1]{0:T(128)} %bitcast.part_ref, ...), custom_call_target="tpu_custom_call" | custom-call | flops 3221225472 | bytes 26346500 | tf_op jit(solution)/shard_map/chunk/pallas_call | solution.py:231
  80.5 1.8 collective-permute-done.21.refs_3_
  83.4 1.6 collective-permute-start.51
  86.5 10.5 %collective-permute-done.52.refs_2_ = bf16[2,64,2048]{2,1,0:T(8,128)(2,1)S(1)} collective-permute-done((bf16[2,64,2048]{2,1,0:T(8,128)(2,1)}, bf16[2,64,2048]{2,1,0:T(8,128)(2,1)S(1)}, u32[]{:S(2)}, u32[]{:S(2)}) %collective-permute-start.52) | collective-permute-done | bytes 524320 | tf_op jit(solution)/shard_map/ppermute | solution.py:148
  98.7 4.2 %collective-permute-done.38.refs_4_ = bf16[64,2048]{1,0:T(8,128)(2,1)S(1)} collective-permute-done((bf16[64,2048]{1,0:T(8,128)(2,1)S(1)}, bf16[64,2048]{1,0:T(8,128)(2,1)S(1)}, u32[]{:S(2)}, u32[]{:S(2)}) %collective-permute-start.38) | collective-permute-done | bytes 262176 | tf_op jit(solution)/shard_map/ppermute | solution.py:148
  108.3 12.2 %chunk.5 = (bf16[2,2,2,128,1024]{4,3,2,1,0:T(8,128)(2,1)}, bf16[2,2,2,128,1024]{4,3,2,1,0:T(8,128)(2,1)}, bf16[1024,2048]{1,0:T(8,128)(2,1)}, bf16[1024,2048]{1,...) custom-call(s32[1]{0:T(128)} %bitcast.part_ref, ...), custom_call_target="tpu_custom_call", output_to_operand_aliasing={{2}: (17, {}), {3}: (18, {}), {4}: (19, {}), {5}: (20, {}),... | custom-call | flops 3221225472 | bytes 37880836 | tf_op jit(solution)/shard_map/chunk/pallas_call | solution.py:231
  122.6 12.1 %chunk.6 = (bf16[2,2,2,128,1024]{4,3,2,1,0:T(8,128)(2,1)}, bf16[2,2,2,128,1024]{4,3,2,1,0:T(8,128)(2,1)}, bf16[1024,2048]{1,0:T(8,128)(2,1)}, bf16[1024,2048]{1,...) custom-call(s32[1]{0:T(128)} %bitcast.part_ref, ...), custom_call_target="tpu_custom_call", output_to_operand_aliasing={{2}: (17, {}), {3}: (18, {}), {4}: (19, {}), {5}: (20, {}),... | custom-call | flops 3221225472 | bytes 37880836 | tf_op jit(solution)/shard_map/chunk/pallas_call | solution.py:231
  136.9 12.2 %chunk.7 = (bf16[2,2,2,128,1024]{4,3,2,1,0:T(8,128)(2,1)}, bf16[2,2,2,128,1024]{4,3,2,1,0:T(8,128)(2,1)}, bf16[1024,2048]{1,0:T(8,128)(2,1)}, bf16[1024,2048]{1,...) custom-call(s32[1]{0:T(128)} %bitcast.part_ref, ...), custom_call_target="tpu_custom_call", output_to_operand_aliasing={{2}: (17, {}), {3}: (18, {}), {4}: (19, {}), {5}: (20, {}),... | custom-call | flops 3221225472 | bytes 37880836 | tf_op jit(solution)/shard_map/chunk/pallas_call | solution.py:231
  151.0 1.6 copy-done.1
  152.5 1.6 copy-done.3
  157.5 2.7 %add_cores.6 = (bf16[2,128,1024]{2,1,0:T(8,128)(2,1)}, bf16[2,128,1024]{2,1,0:T(8,128)(2,1)}, bf16[2,2,128,1024]{3,2,1,0:T(8,128)(2,1)S(1)}) custom-call(bf16[2,2,2,128,1024]{4,3,2,1,0:T(8,128)(2,1)S(1)} %copy-done.5, bf16[2,2,2,128,1024]{4,3,2,1,0:T(8,128)(2,1)} %collective-permute-done.44.got), custom_call_target="tpu_custom_call" | custom-call | bytes 6291456 | tf_op jit(solution)/shard_map/add_cores/pallas_call | solution.py:231
  164.6 2.2 add_cores.4
  166.8 3.7 %collective-permute-done.29.away_out = bf16[2,128,1024]{2,1,0:T(8,128)(2,1)S(1)} collective-permute-done((bf16[2,128,1024]{2,1,0:T(8,128)(2,1)}, bf16[2,128,1024]{2,1,0:T(8,128)(2,1)S(1)}, u32[]{:S(2)}, u32[]{:S(2)}) %collective-permute-start.29) | collective-permute-done | bytes 524320 | tf_op jit(solution)/shard_map/ppermute | solution.py:148
  175.2 2.3 add_cores.7
  177.5 4.2 %collective-permute-done.45.away_out = bf16[2,128,1024]{2,1,0:T(8,128)(2,1)S(1)} collective-permute-done((bf16[2,128,1024]{2,1,0:T(8,128)(2,1)}, bf16[2,128,1024]{2,1,0:T(8,128)(2,1)S(1)}, u32[]{:S(2)}, u32[]{:S(2)}) %collective-permute-start.45) | collective-permute-done | bytes 524320 | tf_op jit(solution)/shard_map/ppermute | solution.py:148
  183.8 3.8 %fusion = bf16[1,2048,512]{2,1,0:T(8,128)(2,1)} fusion(bf16[1024,2048]{1,0:T(8,128)(2,1)S(1)} %copy-done.10, bf16[1024,512]{1,0:T(8,128)(2,1)S(1)} %copy-done.13, f32[]{:T(128)S(6)} %div.3), kind=kOutput, calls=%fused_computation.3 | convolution fusion | flops 2149580800 | bytes 7340036 | tf_op jit(solution)/shard_map/dot_general | solution.py:202
  188.9 14.5 %collective-permute-done.61.away_out = bf16[2,128,1024]{2,1,0:T(8,128)(2,1)S(1)} collective-permute-done((bf16[2,128,1024]{2,1,0:T(8,128)(2,1)S(1)}, bf16[2,128,1024]{2,1,0:T(8,128)(2,1)S(1)}, u32[]{:S(2)}, u32[]{:S(2)}) %collective-permute-start.61) | collective-permute-done | bytes 524320 | tf_op jit(solution)/shard_map/ppermute | solution.py:148
  204.6 5.3 %collective-permute-done.62.away_grad = bf16[2,128,1024]{2,1,0:T(8,128)(2,1)S(1)} collective-permute-done((bf16[2,128,1024]{2,1,0:T(8,128)(2,1)S(1)}, bf16[2,128,1024]{2,1,0:T(8,128)(2,1)S(1)}, u32[]{:S(2)}, u32[]{:S(2)}) %collective-permute-start.62) | collective-permute-done | bytes 524320 | tf_op jit(solution)/shard_map/ppermute | solution.py:148
  214.2 3.8 %fusion.1 = bf16[1,2048,512]{2,1,0:T(8,128)(2,1)} fusion(bf16[1024,2048]{1,0:T(8,128)(2,1)S(1)} %copy-done.10, bf16[1024,512]{1,0:T(8,128)(2,1)S(1)} %copy-done.14, f32[]{:T(128)S(6)} %div.3), kind=kOutput, calls=%fused_computation.4 | convolution fusion | flops 2149580800 | bytes 7340036 | tf_op jit(solution)/shard_map/dot_general | solution.py:202
  218.9 1.6 add_last.5
  221.3 3.5 %collective-permute-start.33 = (bf16[2,128,1024]{2,1,0:T(8,128)(2,1)S(1)}, bf16[2,128,1024]{2,1,0:T(8,128)(2,1)S(1)}, u32[]{:S(2)}, u32[]{:S(2)}) collective-permute-start(bf16[2,128,1024]{2,1,0:T(8,128)(2,1)S(1)} %add_last.5), channel_id=1, source_target_pairs={{0,24},{2,26},{4,28},{6,30},{8,0},{10,2},{12,4},{14,6},{16,8},{18,... | collective-permute-start | bytes 1572872 | tf_op jit(solution)/shard_map/ppermute | solution.py:153
  226.7 2.3 collective-permute-start.65
  229.1 3.8 %fusion.2 = bf16[1,512,2048]{2,1,0:T(8,128)(2,1)} fusion(bf16[1024,512]{1,0:T(8,128)(2,1)S(1)} %copy-done.12, bf16[1024,2048]{1,0:T(8,128)(2,1)S(1)} %copy-done.11, f32[]{:T(128)S(6)} %div.3), kind=kOutput, calls=%fused_computation.5 | convolution fusion | flops 2149580800 | bytes 7340036 | tf_op jit(solution)/shard_map/dot_general | solution.py:202
  233.0 4.2 %collective-permute-done.33 = bf16[2,128,1024]{2,1,0:T(8,128)(2,1)S(1)} collective-permute-done((bf16[2,128,1024]{2,1,0:T(8,128)(2,1)S(1)}, bf16[2,128,1024]{2,1,0:T(8,128)(2,1)S(1)}, u32[]{:S(2)}, u32[]{:S(2)}) %collective-permute-start.33) | collective-permute-done | bytes 524320 | tf_op jit(solution)/shard_map/ppermute | solution.py:153
  237.2 29.8 %collective-permute-done.49 = bf16[2,128,1024]{2,1,0:T(8,128)(2,1)S(1)} collective-permute-done((bf16[2,128,1024]{2,1,0:T(8,128)(2,1)S(1)}, bf16[2,128,1024]{2,1,0:T(8,128)(2,1)S(1)}, u32[]{:S(2)}, u32[]{:S(2)}) %collective-permute-start.49) | collective-permute-done | bytes 524320 | tf_op jit(solution)/shard_map/ppermute | solution.py:153
  (230 shorter events, 69.8 us)
Async XLA Ops:
  18.0 16.4 %collective-permute-start.18 = (bf16[2,64,2048]{2,1,0:T(8,128)(2,1)S(1)}, bf16[2,64,2048]{2,1,0:T(8,128)(2,1)S(1)}, u32[]{:S(2)}, u32[]{:S(2)}) collective-permute-start(bf16[2,64,2048]{2,1,0:T(8,128)(2,1)S(1)} %get-tuple-element.55.refs_0_), channel_id=1, source_target_pairs={{0,8},{2,10},{4,12},{6,14},{8,16},{10,18},{12,20},{14,22},{16,24},... | collective-permute-start | bytes 1572872 | tf_op jit(solution)/shard_map/ppermute | solution.py:153
  18.1 20.6 %collective-permute-start.8 = (bf16[2,64,2048]{2,1,0:T(8,128)(2,1)S(1)}, bf16[2,64,2048]{2,1,0:T(8,128)(2,1)}, u32[]{:S(2)}, u32[]{:S(2)}) collective-permute-start(bf16[2,64,2048]{2,1,0:T(8,128)(2,1)S(1)} %get-tuple-element.55.refs_0_), channel_id=1, source_target_pairs={{0,2},{2,0},{4,6},{6,4},{8,10},{10,8},{12,14},{14,12},{16,18},{18,... | collective-permute-start | bytes 1572872 | tf_op jit(solution)/shard_map/ppermute | solution.py:148
  18.6 17.3 %collective-permute-start.5 = (bf16[2,64,2048]{2,1,0:T(8,128)(2,1)S(1)}, bf16[2,64,2048]{2,1,0:T(8,128)(2,1)S(1)}, u32[]{:S(2)}, u32[]{:S(2)}) collective-permute-start(bf16[2,64,2048]{2,1,0:T(8,128)(2,1)S(1)} %get-tuple-element.55.refs_0_), channel_id=1, source_target_pairs={{0,4},{2,6},{4,0},{6,2},{8,12},{10,14},{12,8},{14,10},{16,20},{18,... | collective-permute-start | bytes 1572872 | tf_op jit(solution)/shard_map/ppermute | solution.py:148
  20.1 18.5 %collective-permute-start.9 = (bf16[2,64,2048]{2,1,0:T(8,128)(2,1)S(1)}, bf16[2,64,2048]{2,1,0:T(8,128)(2,1)}, u32[]{:S(2)}, u32[]{:S(2)}) collective-permute-start(bf16[2,64,2048]{2,1,0:T(8,128)(2,1)S(1)} %get-tuple-element.56.refs_1_), channel_id=1, source_target_pairs={{0,2},{2,0},{4,6},{6,4},{8,10},{10,8},{12,14},{14,12},{16,18},{18,... | collective-permute-start | bytes 1572872 | tf_op jit(solution)/shard_map/ppermute | solution.py:148
  38.5 23.2 %collective-permute-start.34 = (bf16[2,64,2048]{2,1,0:T(8,128)(2,1)S(1)}, bf16[2,64,2048]{2,1,0:T(8,128)(2,1)}, u32[]{:S(2)}, u32[]{:S(2)}) collective-permute-start(bf16[2,64,2048]{2,1,0:T(8,128)(2,1)S(1)} %collective-permute-done.18.refs_0_), channel_id=1, source_target_pairs={{0,8},{2,10},{4,12},{6,14},{8,16},{10,18},{12,20},{14,22},{16,24},... | collective-permute-start | bytes 1572872 | tf_op jit(solution)/shard_map/ppermute | solution.py:153
  38.6 23.6 %collective-permute-start.23 = (bf16[2,64,2048]{2,1,0:T(8,128)(2,1)S(1)}, bf16[2,64,2048]{2,1,0:T(8,128)(2,1)S(1)}, u32[]{:S(2)}, u32[]{:S(2)}) collective-permute-start(bf16[2,64,2048]{2,1,0:T(8,128)(2,1)S(1)} %collective-permute-done.18.refs_0_), channel_id=1, source_target_pairs={{0,2},{2,0},{4,6},{6,4},{8,10},{10,8},{12,14},{14,12},{16,18},{18,... | collective-permute-start | bytes 1572872 | tf_op jit(solution)/shard_map/ppermute | solution.py:148
  38.7 23.7 %collective-permute-start.19 = (bf16[2,64,2048]{2,1,0:T(8,128)(2,1)S(1)}, bf16[2,64,2048]{2,1,0:T(8,128)(2,1)S(1)}, u32[]{:S(2)}, u32[]{:S(2)}) collective-permute-start(bf16[2,64,2048]{2,1,0:T(8,128)(2,1)S(1)} %collective-permute-done.18.refs_0_), channel_id=1, source_target_pairs={{0,1},{1,0},{2,3},{3,2},{4,5},{5,4},{6,7},{7,6},{8,9},{9,8},{10,11... | collective-permute-start | bytes 1572872 | tf_op jit(solution)/shard_map/ppermute | solution.py:148
  48.2 18.5 %collective-permute-start.10 = (bf16[2,64,2048]{2,1,0:T(8,128)(2,1)}, bf16[2,64,2048]{2,1,0:T(8,128)(2,1)S(1)}, u32[]{:S(2)}, u32[]{:S(2)}) collective-permute-start(bf16[2,64,2048]{2,1,0:T(8,128)(2,1)} %copy-done.28), channel_id=1, source_target_pairs={{0,2},{2,0},{4,6},{6,4},{8,10},{10,8},{12,14},{14,12},{16,18},{18,... | collective-permute-start | bytes 1572872 | tf_op jit(solution)/shard_map/ppermute | solution.py:148
  62.2 20.1 %collective-permute-start.50 = (bf16[2,64,2048]{2,1,0:T(8,128)(2,1)}, bf16[2,64,2048]{2,1,0:T(8,128)(2,1)}, u32[]{:S(2)}, u32[]{:S(2)}) collective-permute-start(bf16[2,64,2048]{2,1,0:T(8,128)(2,1)} %collective-permute-done.34.refs_0_), channel_id=1, source_target_pairs={{0,8},{2,10},{4,12},{6,14},{8,16},{10,18},{12,20},{14,22},{16,24},... | collective-permute-start | bytes 1572872 | tf_op jit(solution)/shard_map/ppermute | solution.py:153
  62.4 20.4 %collective-permute-start.36 = (bf16[2,64,2048]{2,1,0:T(8,128)(2,1)}, bf16[2,64,2048]{2,1,0:T(8,128)(2,1)S(1)}, u32[]{:S(2)}, u32[]{:S(2)}) collective-permute-start(bf16[2,64,2048]{2,1,0:T(8,128)(2,1)} %collective-permute-done.34.refs_0_), channel_id=1, source_target_pairs={{0,4},{2,6},{4,0},{6,2},{8,12},{10,14},{12,8},{14,10},{16,20},{18,... | collective-permute-start | bytes 1572872 | tf_op jit(solution)/shard_map/ppermute | solution.py:148
  63.7 16.6 %collective-permute-start.22 = (bf16[64,2048]{1,0:T(8,128)(2,1)}, bf16[64,2048]{1,0:T(8,128)(2,1)S(1)}, u32[]{:S(2)}, u32[]{:S(2)}) collective-permute-start(bf16[64,2048]{1,0:T(8,128)(2,1)} %slice_bitcast_fusion.6), channel_id=1, source_target_pairs={{0,1},{1,0},{2,3},{3,2},{4,5},{5,4},{6,7},{7,6},{8,9},{9,8},{10,11... | collective-permute-start | bytes 786440 | tf_op jit(solution)/shard_map/ppermute | solution.py:148
  65.2 17.1 %collective-permute-start.21 = (bf16[64,2048]{1,0:T(8,128)(2,1)}, bf16[64,2048]{1,0:T(8,128)(2,1)}, u32[]{:S(2)}, u32[]{:S(2)}) collective-permute-start(bf16[64,2048]{1,0:T(8,128)(2,1)} %slice_bitcast_fusion.7), channel_id=1, source_target_pairs={{0,4},{2,6},{4,0},{6,2},{8,12},{10,14},{12,8},{14,10},{16,20},{18,... | collective-permute-start | bytes 786440 | tf_op jit(solution)/shard_map/ppermute | solution.py:148
  83.4 21.0 %collective-permute-start.51 = (bf16[2,64,2048]{2,1,0:T(8,128)(2,1)}, bf16[2,64,2048]{2,1,0:T(8,128)(2,1)S(1)}, u32[]{:S(2)}, u32[]{:S(2)}) collective-permute-start(bf16[2,64,2048]{2,1,0:T(8,128)(2,1)} %collective-permute-done.50.refs_0_), channel_id=1, source_target_pairs={{0,1},{1,0},{2,3},{3,2},{4,5},{5,4},{6,7},{7,6},{8,9},{9,8},{10,11... | collective-permute-start | bytes 1572872 | tf_op jit(solution)/shard_map/ppermute | solution.py:148
  85.6 17.3 %collective-permute-start.38 = (bf16[64,2048]{1,0:T(8,128)(2,1)S(1)}, bf16[64,2048]{1,0:T(8,128)(2,1)S(1)}, u32[]{:S(2)}, u32[]{:S(2)}) collective-permute-start(bf16[64,2048]{1,0:T(8,128)(2,1)S(1)} %slice_bitcast_fusion.4), channel_id=1, source_target_pairs={{0,1},{1,0},{2,3},{3,2},{4,5},{5,4},{6,7},{7,6},{8,9},{9,8},{10,11... | collective-permute-start | bytes 786440 | tf_op jit(solution)/shard_map/ppermute | solution.py:148
  98.2 22.4 %collective-permute-start.55 = (bf16[2,64,2048]{2,1,0:T(8,128)(2,1)}, bf16[2,64,2048]{2,1,0:T(8,128)(2,1)S(1)}, u32[]{:S(2)}, u32[]{:S(2)}) collective-permute-start(bf16[2,64,2048]{2,1,0:T(8,128)(2,1)} %collective-permute-done.50.refs_0_), channel_id=1, source_target_pairs={{0,2},{2,0},{4,6},{6,4},{8,10},{10,8},{12,14},{14,12},{16,18},{18,... | collective-permute-start | bytes 1572872 | tf_op jit(solution)/shard_map/ppermute | solution.py:148
  98.3 23.2 %collective-permute-start.41 = (bf16[2,64,2048]{2,1,0:T(8,128)(2,1)S(1)}, bf16[2,64,2048]{2,1,0:T(8,128)(2,1)}, u32[]{:S(2)}, u32[]{:S(2)}) collective-permute-start(bf16[2,64,2048]{2,1,0:T(8,128)(2,1)S(1)} %collective-permute-done.36.refs_2_), channel_id=1, source_target_pairs={{0,2},{2,0},{4,6},{6,4},{8,10},{10,8},{12,14},{14,12},{16,18},{18,... | collective-permute-start | bytes 1572872 | tf_op jit(solution)/shard_map/ppermute | solution.py:148
  102.9 19.0 %collective-permute-start.40 = (bf16[2,64,2048]{2,1,0:T(8,128)(2,1)S(1)}, bf16[2,64,2048]{2,1,0:T(8,128)(2,1)}, u32[]{:S(2)}, u32[]{:S(2)}) collective-permute-start(bf16[2,64,2048]{2,1,0:T(8,128)(2,1)S(1)} %collective-permute-done.35.refs_1_), channel_id=1, source_target_pairs={{0,2},{2,0},{4,6},{6,4},{8,10},{10,8},{12,14},{14,12},{16,18},{18,... | collective-permute-start | bytes 1572872 | tf_op jit(solution)/shard_map/ppermute | solution.py:148
  106.0 16.1 %collective-permute-start.54 = (bf16[64,2048]{1,0:T(8,128)(2,1)}, bf16[64,2048]{1,0:T(8,128)(2,1)}, u32[]{:S(2)}, u32[]{:S(2)}) collective-permute-start(bf16[64,2048]{1,0:T(8,128)(2,1)} %slice_bitcast_fusion.2), channel_id=1, source_target_pairs={{0,1},{1,0},{2,3},{3,2},{4,5},{5,4},{6,7},{7,6},{8,9},{9,8},{10,11... | collective-permute-start | bytes 786440 | tf_op jit(solution)/shard_map/ppermute | solution.py:148
  121.5 28.2 %collective-permute-start.28 = (bf16[2,2,2,128,1024]{4,3,2,1,0:T(8,128)(2,1)}, bf16[2,2,2,128,1024]{4,3,2,1,0:T(8,128)(2,1)S(1)}, u32[]{:S(2)}, u32[]{:S(2)}) collective-permute-start(bf16[2,2,2,128,1024]{4,3,2,1,0:T(8,128)(2,1)} %get-tuple-element.70), channel_id=1, source_target_pairs={{0,2},{2,0},{4,6},{6,4},{8,10},{10,8},{12,14},{14,12},{16,18},{18,... | collective-permute-start | bytes 6291464 | tf_op jit(solution)/shard_map/ppermute | solution.py:148
  134.7 22.8 %collective-permute-start.44 = (bf16[2,2,2,128,1024]{4,3,2,1,0:T(8,128)(2,1)}, bf16[2,2,2,128,1024]{4,3,2,1,0:T(8,128)(2,1)}, u32[]{:S(2)}, u32[]{:S(2)}) collective-permute-start(bf16[2,2,2,128,1024]{4,3,2,1,0:T(8,128)(2,1)} %get-tuple-element.82), channel_id=1, source_target_pairs={{0,2},{2,0},{4,6},{6,4},{8,10},{10,8},{12,14},{14,12},{16,18},{18,... | collective-permute-start | bytes 6291464 | tf_op jit(solution)/shard_map/ppermute | solution.py:148
  135.2 25.7 %collective-permute-start.13 = (bf16[2,2,2,128,1024]{4,3,2,1,0:T(8,128)(2,1)}, bf16[2,2,2,128,1024]{4,3,2,1,0:T(8,128)(2,1)}, u32[]{:S(2)}, u32[]{:S(2)}) collective-permute-start(bf16[2,2,2,128,1024]{4,3,2,1,0:T(8,128)(2,1)} %get-tuple-element.58), channel_id=1, source_target_pairs={{0,2},{2,0},{4,6},{6,4},{8,10},{10,8},{12,14},{14,12},{16,18},{18,... | collective-permute-start | bytes 6291464 | tf_op jit(solution)/shard_map/ppermute | solution.py:148
  149.2 24.6 %collective-permute-start.60 = (bf16[2,2,2,128,1024]{4,3,2,1,0:T(8,128)(2,1)}, bf16[2,2,2,128,1024]{4,3,2,1,0:T(8,128)(2,1)}, u32[]{:S(2)}, u32[]{:S(2)}) collective-permute-start(bf16[2,2,2,128,1024]{4,3,2,1,0:T(8,128)(2,1)} %get-tuple-element.94), channel_id=1, source_target_pairs={{0,2},{2,0},{4,6},{6,4},{8,10},{10,8},{12,14},{14,12},{16,18},{18,... | collective-permute-start | bytes 6291464 | tf_op jit(solution)/shard_map/ppermute | solution.py:148
  160.1 21.6 %collective-permute-start.45 = (bf16[2,128,1024]{2,1,0:T(8,128)(2,1)}, bf16[2,128,1024]{2,1,0:T(8,128)(2,1)S(1)}, u32[]{:S(2)}, u32[]{:S(2)}) collective-permute-start(bf16[2,128,1024]{2,1,0:T(8,128)(2,1)} %get-tuple-element.84), channel_id=1, source_target_pairs={{0,4},{2,6},{4,0},{6,2},{8,12},{10,14},{12,8},{14,10},{16,20},{18,... | collective-permute-start | bytes 1572872 | tf_op jit(solution)/shard_map/ppermute | solution.py:148
  160.9 22.3 %collective-permute-start.46 = (bf16[2,128,1024]{2,1,0:T(8,128)(2,1)}, bf16[2,128,1024]{2,1,0:T(8,128)(2,1)}, u32[]{:S(2)}, u32[]{:S(2)}) collective-permute-start(bf16[2,128,1024]{2,1,0:T(8,128)(2,1)} %get-tuple-element.85), channel_id=1, source_target_pairs={{0,1},{1,0},{2,3},{3,2},{4,5},{5,4},{6,7},{7,6},{8,9},{9,8},{10,11... | collective-permute-start | bytes 1572872 | tf_op jit(solution)/shard_map/ppermute | solution.py:148
  170.5 40.3 %collective-permute-start.14 = (bf16[2,128,1024]{2,1,0:T(8,128)(2,1)S(1)}, bf16[2,128,1024]{2,1,0:T(8,128)(2,1)S(1)}, u32[]{:S(2)}, u32[]{:S(2)}) collective-permute-start(bf16[2,128,1024]{2,1,0:T(8,128)(2,1)S(1)} %get-tuple-element.60), channel_id=1, source_target_pairs={{0,4},{2,6},{4,0},{6,2},{8,12},{10,14},{12,8},{14,10},{16,20},{18,... | collective-permute-start | bytes 1572872 | tf_op jit(solution)/shard_map/ppermute | solution.py:148
  171.9 39.6 %collective-permute-start.15 = (bf16[2,128,1024]{2,1,0:T(8,128)(2,1)S(1)}, bf16[2,128,1024]{2,1,0:T(8,128)(2,1)S(1)}, u32[]{:S(2)}, u32[]{:S(2)}) collective-permute-start(bf16[2,128,1024]{2,1,0:T(8,128)(2,1)S(1)} %get-tuple-element.61), channel_id=1, source_target_pairs={{0,1},{1,0},{2,3},{3,2},{4,5},{5,4},{6,7},{7,6},{8,9},{9,8},{10,11... | collective-permute-start | bytes 1572872 | tf_op jit(solution)/shard_map/ppermute | solution.py:148
  173.8 39.1 %collective-permute-start.31 = (bf16[128,1024]{1,0:T(8,128)(2,1)S(1)}, bf16[128,1024]{1,0:T(8,128)(2,1)S(1)}, u32[]{:S(2)}, u32[]{:S(2)}) collective-permute-start(bf16[128,1024]{1,0:T(8,128)(2,1)S(1)} %get-tuple-element.74), channel_id=1, source_target_pairs={{0,1},{1,0},{2,3},{3,2},{4,5},{5,4},{6,7},{7,6},{8,9},{9,8},{10,11... | collective-permute-start | bytes 786440 | tf_op jit(solution)/shard_map/ppermute | solution.py:148
  181.7 21.6 %collective-permute-start.61 = (bf16[2,128,1024]{2,1,0:T(8,128)(2,1)S(1)}, bf16[2,128,1024]{2,1,0:T(8,128)(2,1)S(1)}, u32[]{:S(2)}, u32[]{:S(2)}) collective-permute-start(bf16[2,128,1024]{2,1,0:T(8,128)(2,1)S(1)} %get-tuple-element.96), channel_id=1, source_target_pairs={{0,4},{2,6},{4,0},{6,2},{8,12},{10,14},{12,8},{14,10},{16,20},{18,... | collective-permute-start | bytes 1572872 | tf_op jit(solution)/shard_map/ppermute | solution.py:148
  183.2 26.8 %collective-permute-start.62 = (bf16[2,128,1024]{2,1,0:T(8,128)(2,1)S(1)}, bf16[2,128,1024]{2,1,0:T(8,128)(2,1)S(1)}, u32[]{:S(2)}, u32[]{:S(2)}) collective-permute-start(bf16[2,128,1024]{2,1,0:T(8,128)(2,1)S(1)} %get-tuple-element.97), channel_id=1, source_target_pairs={{0,1},{1,0},{2,3},{3,2},{4,5},{5,4},{6,7},{7,6},{8,9},{9,8},{10,11... | collective-permute-start | bytes 1572872 | tf_op jit(solution)/shard_map/ppermute | solution.py:148
  221.3 15.9 %collective-permute-start.33 = (bf16[2,128,1024]{2,1,0:T(8,128)(2,1)S(1)}, bf16[2,128,1024]{2,1,0:T(8,128)(2,1)S(1)}, u32[]{:S(2)}, u32[]{:S(2)}) collective-permute-start(bf16[2,128,1024]{2,1,0:T(8,128)(2,1)S(1)} %add_last.5), channel_id=1, source_target_pairs={{0,24},{2,26},{4,28},{6,30},{8,0},{10,2},{12,4},{14,6},{16,8},{18,... | collective-permute-start | bytes 1572872 | tf_op jit(solution)/shard_map/ppermute | solution.py:153
  226.1 41.0 %collective-permute-start.49 = (bf16[2,128,1024]{2,1,0:T(8,128)(2,1)S(1)}, bf16[2,128,1024]{2,1,0:T(8,128)(2,1)S(1)}, u32[]{:S(2)}, u32[]{:S(2)}) collective-permute-start(bf16[2,128,1024]{2,1,0:T(8,128)(2,1)S(1)} %add_last.6), channel_id=1, source_target_pairs={{0,16},{2,18},{4,20},{6,22},{8,24},{10,26},{12,28},{14,30},{16,0},... | collective-permute-start | bytes 1572872 | tf_op jit(solution)/shard_map/ppermute | solution.py:153
  226.7 40.3 %collective-permute-start.65 = (bf16[2,128,1024]{2,1,0:T(8,128)(2,1)S(1)}, bf16[2,128,1024]{2,1,0:T(8,128)(2,1)S(1)}, u32[]{:S(2)}, u32[]{:S(2)}) collective-permute-start(bf16[2,128,1024]{2,1,0:T(8,128)(2,1)S(1)} %add_last.7), channel_id=1, source_target_pairs={{0,8},{2,10},{4,12},{6,14},{8,16},{10,18},{12,20},{14,22},{16,24},... | collective-permute-start | bytes 1572872 | tf_op jit(solution)/shard_map/ppermute | solution.py:153
  (74 other events, 929.1 us)
